TPU v7x, 1024 devices: a whole 4x4x32 slice. The times are simulated.
1024 devices in a mesh: space: 32 (over y, z_lo), chan: 8 (over x, core), filt: 4 (over z_hi).
Axes of the slice: x: 4, y: 4, z: 32 (z_hi: 4, z_lo: 8; z = z_hi * 8 + z_lo), core: 2. Of those that a mesh axis runs over, the one named last changes fastest.
Arguments:
- activations: bfloat16 [256, 128, 4, 128], P('chan', 'space'), may hold values from -6 to 6
- out_grad: bfloat16 [4, 64, 128, 4, 128], P('filt', 'chan', 'space'), may hold values from -6 to 6
- weight: bfloat16 [27, 256, 256], P(None, 'chan', 'filt'), may hold values from -0.078125 to 0.078125
Outputs:
- grad_input: bfloat16 [256, 128, 4, 128], P(('chan', 'filt'), 'space')
- grad_weight: float32 [27, 256, 256], P(None, 'chan', 'filt')
All inputs are finite; a program needn't handle non-finite values.
Results may differ from a plain program's by a relative error of at most 0.001.
Values may be sent and summed in bfloat16 or wider, within the bound.
A program may use at most 32 MiB of HBM per device.

v0:
```python
import math

import jax
import jax.numpy as jnp
from jax import lax
from jax.sharding import PartitionSpec as P


def extended(block, sides, width):
    for axis, dim in sides:
        count = lax.axis_size(axis)
        forward = [(i, i + 1) for i in range(count - 1)]
        backward = [(target, source) for source, target in forward]
        low = lax.ppermute(
            lax.slice_in_dim(block, block.shape[dim] - width, None, axis=dim), axis, forward
        )
        high = lax.ppermute(lax.slice_in_dim(block, 0, width, axis=dim), axis, backward)
        block = jnp.concatenate([low, block, high], axis=dim)
    return block


def body(activations, out_grad, weight):
    chan_here, count_x, count_z, count_y = activations.shape
    grad_full = lax.all_gather(out_grad, "chan", axis=1, tiled=True)
    margined = extended(grad_full, (("space", 2),), 1)
    margined = margined[0]
    filt_here = margined.shape[0]
    padded = jnp.pad(margined, ((0, 0), (0, 0), (1, 1), (1, 1)))
    cells_here = count_x * count_y * count_z
    flat_act = activations.reshape(chan_here, cells_here)
    term = jnp.zeros((chan_here, cells_here), jnp.float32)
    tap_grads = []
    for shift_x in range(3):
        for shift_y in range(3):
            for shift_z in range(3):
                tap_index = (shift_x * 3 + shift_y) * 3 + shift_z
                shifted = padded[
                    :,
                    2 - shift_x : 2 - shift_x + count_x,
                    2 - shift_z : 2 - shift_z + count_z,
                    2 - shift_y : 2 - shift_y + count_y,
                ].reshape(filt_here, cells_here)
                term = term + jnp.dot(
                    weight[tap_index], shifted, preferred_element_type=jnp.float32
                )
                tap_grads.append(
                    lax.dot_general(
                        flat_act,
                        shifted,
                        (((1,), (1,)), ((), ())),
                        preferred_element_type=jnp.float32,
                    )
                )
    total_cells = count_x * lax.axis_size("space") * count_y * count_z
    cell_scale = 1.0 / math.sqrt(total_cells)
    local_taps = jnp.stack(tap_grads, axis=0) * jnp.float32(cell_scale)
    grad_weight = lax.psum(local_taps, "space")
    term = term.reshape(chan_here, count_x, count_z, count_y)
    summed = lax.psum_scatter(term, "filt", scatter_dimension=0, tiled=True)
    return (summed.astype(jnp.bfloat16), grad_weight)


def solution(mesh):
    return jax.shard_map(
        body,
        mesh=mesh,
        in_specs=(
            P("chan", "space", None, None),
            P("filt", "chan", "space", None, None),
            P(None, "chan", "filt"),
        ),
        out_specs=(P(("chan", "filt"), "space", None, None), P(None, "chan", "filt")),
        check_vma=False,
    )
```

profile of v0, /device:TPU:6, one launch (start us, length us, event | category | flops | bytes accessed | tf_op | source)
XLA Modules:
  0.0 536.0 jit_solution(18234023534557387386)
XLA Ops:
  8.0 21.4 %all_gather.3 = bf16[1,64,4,4,128]{4,1,3,2,0:T(8,128)(2,1)S(1)} all-gather(bf16[1,8,4,4,128]{4,1,3,2,0:T(8,128)(2,1)S(1)} %copy.88), channel_id=1, replica_groups=mesh['space'=32,'chan'=8,'filt'=4] {'chan'}, dimensions={1}, use_global_device_ids=true | all-gather | bytes 294912 | tf_op jit(solution)/shard_map/all_gather | solution.py:24
  33.9 3.0 collective-permute-done.1
  37.0 3.2 pad_slice_fusion.8
  53.8 1.9 copy.96
  56.8 1.9 copy.97
  60.4 1.9 copy.98
  64.1 1.9 copy.99
  66.0 1.9 reshape.99
  67.8 1.9 copy.100
  69.7 1.8 reshape.100
  71.5 1.9 copy.101
  77.2 1.9 copy.103
  80.9 1.9 copy.104
  82.8 1.9 reshape.104
  84.6 1.9 copy.105
  88.3 1.9 copy.110
  90.1 2.0 reshape.110
  92.2 1.9 fusion.64
  96.5 1.8 reshape.109
  98.4 1.9 convolution_bitcast_fusion.6
  101.2 1.8 reshape.108
  103.0 1.9 convolution_bitcast_fusion.7
  105.8 1.8 reshape.107
  107.6 1.9 convolution_bitcast_fusion.8
  110.4 1.9 reshape.106
  113.2 1.8 reshape.115
  117.1 1.8 reshape.114
  121.0 1.8 reshape.113
  124.9 1.8 reshape.112
  128.8 1.9 reshape.111
  142.3 62.8 %all-reduce.6 = bf16[32,4,4,128]{3,2,1,0:T(4,128)(2,1)S(1)} all-reduce(f32[32,4,4,128]{3,2,1,0:T(4,128)S(1)} %reshape.116), channel_id=2, replica_groups=mesh['space'=32,'chan'=8,'filt'=4] {'filt'}, use_global_device_ids=true, to_apply=%region_0.1.clone | all-reduce | flops 65536 | bytes 393216
  205.7 321.6 %all-reduce.5.cloned.1.call-done = f32[27,32,64]{2,1,0:T(8,128)} async-done(((f32[27,32,64]{2,1,0:T(8,128)}), f32[27,32,64]{2,1,0:T(8,128)}) %all-reduce.5.cloned.1.call-update) | async-done | bytes 221200 | tf_op jit(solution)/shard_map/psum | solution.py:57
  (139 shorter events, 58.7 us)
Async XLA Ops:
  7.2 33.5 %copy-start = (bf16[32,4,4,128]{3,2,1,0:T(4,128)(2,1)S(1)}, bf16[32,4,4,128]{3,2,1,0:T(4,128)(2,1)}, u32[]{:S(2)}) copy-start(bf16[32,4,4,128]{3,2,1,0:T(4,128)(2,1)} %param.3) | copy-start | bytes 393220
  7.2 520.1 %all-reduce.5.cloned.1.call-start = ((), (), s32[]{:S(2)}) async-start(), calls=%async_computation | async-start | bytes 884736 | tf_op jit(solution)/shard_map/psum | solution.py:57
  29.4 4.5 collective-permute-start
  30.7 6.2 %collective-permute-start.1 = (bf16[1,64,1,4,128]{4,1,3,2,0:T(8,128)(2,1)S(1)}, bf16[1,64,1,4,128]{4,1,3,2,0:T(8,128)(2,1)S(1)}, u32[]{:S(2)}, u32[]{:S(2)}) collective-permute-start(bf16[1,64,1,4,128]{4,1,3,2,0:T(8,128)(2,1)S(1)} %get-tuple-element.30), channel_id=1, source_target_pairs={{32,0},{64,32},{96,64},{128,96},{160,128},{192,160},{224,192},{256... | collective-permute-start | bytes 196616 | tf_op jit(solution)/shard_map/ppermute | solution.py:17
  48.4 0.9 copy-start.20
  92.1 1.9 copy-start.15
  92.1 3.5 copy-start.19
  98.4 1.9 copy-start.18
  103.0 1.9 copy-start.17
  107.6 1.9 copy-start.16
  128.8 3.1 copy-start.14
  130.7 1.2 copy-start.21
  132.9 1.0 copy-start.1
  133.9 0.9 copy-start.2
  134.8 1.0 copy-start.3
  135.8 1.0 copy-start.4
  136.7 0.9 copy-start.5
  137.9 1.0 copy-start.6
  138.8 1.0 copy-start.7
  139.8 0.9 copy-start.8
  139.8 1.1 copy-start.12
  139.8 1.1 copy-start.13
  140.7 1.0 copy-start.9
  140.7 1.1 copy-start.10
  140.7 1.1 copy-start.11
Sparse Core Ops, SparseCore 0:
  48.5 478.7 all-reduce.4
where the time goes:
time: 538 us; the launch traced here: 536 us
  waiting for transfers between devices  325 us (60%)
  local copies, waits for them, and re-layouts  84.1 us (16%)
  blocking collectives  84.1 us (16%)
  matrix products  24.5 us (5%)
  between operations  15.1 us (3%)
    psum x1, waiting for transfers between devices, body(): grad_weight = lax.psum(local_taps, 'space')  322 us
    unnamed x1, blocking collectives  62.8 us
    reshape x27, local copies, waits for them, and re-layouts, body(): shifted = padded[:, 2 - shift_x:2 - shift_x + count_x, 2 - shift_z:2 - sh...  37.6 us
    slice x29, local copies, waits for them, and re-layouts, body(): padded[:, 2 - shift_x:2 - shift_x + count_x, 2 - shift_z:2 - shift_z + co...  33.8 us
    all_gather x1, blocking collectives, body(): grad_full = lax.all_gather(out_grad, 'chan', axis=1, tiled=True)  21.4 us
    dot_general x27, matrix products, body(): jnp.dot(weight[tap_index], shifted, preferred_element_type=jnp.float32)  17.7 us
    unnamed x47, local copies, waits for them, and re-layouts  12 us
  transfers between devices with their start and end apart: 3, of which 2 were waited for; matrix products, arithmetic and copies ran while one was open for 16% of the time, Pallas kernels for 0%

commit v1 on v0

v1 whole, which is shorter than its diff:
```python
import functools
import math

import jax
import jax.numpy as jnp
from jax import lax
from jax.experimental import pallas as pl
from jax.experimental.pallas import tpu as pltpu
from jax.sharding import PartitionSpec as P

MESH = pl.DeviceIdType.MESH
F32, BF16 = jnp.float32, jnp.bfloat16
ROWS = 512
TAP_ROWS = 128


def kernel(
    sizes, scale,
    act_ref, shard_ref, taps_ref,
    gi_ref, gw_ref,
    grads, acts, wparts, lhs, acc, mine, from_y, for_z, from_z, total, prod, outs, halo,
    s_own, r_own, s_act, r_act, s_filt, r_filt, s_wf, r_wf, s_wy, r_wy, s_x, r_x, s_sib, r_sib,
    s_yr, r_yr, s_zr, r_zr, s_zg, r_zg, s_yg, r_yg, s_halo, r_halo,
):
    ny, nz, nx, nf = sizes
    nc, ns = nx * 2, ny * nz
    space, chan, filt = lax.axis_index("space"), lax.axis_index("chan"), lax.axis_index("filt")
    row, run = space // nz, space % nz
    chip, core = chan // 2, chan % 2
    sib = chip * 2 + (1 - core)
    shard_rows = shard_ref.shape[0]
    own_filt = shard_rows // 16
    y_rows = ROWS // ny
    z_rows = y_rows // nz
    w_rows = TAP_ROWS // ny
    before, after = (space + ns - 1) % ns, (space + 1) % ns

    def at_y(d):
        return {"space": ((row + d) % ny) * nz + run}

    def at_z(d):
        return {"space": row * nz + (run + d) % nz}

    def at_x(d):
        return {"chan": ((chip + d) % nx) * 2 + core}

    barrier = pltpu.get_barrier_semaphore()
    partners = [{"chan": (chan + d) % nc} for d in range(1, nc)]
    partners += [{"filt": (filt + d) % nf} for d in range(1, nf)]
    partners += [at_y(d) for d in range(1, ny)] + [at_z(d) for d in range(1, nz)]
    partners += [{"space": before}, {"space": after}]
    for partner in partners:
        pl.semaphore_signal(barrier, inc=1, device_id=partner, device_id_type=MESH)

    sent = []

    def remote(src, dst, ssem, rsem, where):
        copy = pltpu.make_async_remote_copy(
            src_ref=src, dst_ref=dst, send_sem=ssem, recv_sem=rsem, device_id=where, device_id_type=MESH
        )
        copy.start()
        sent.append(copy)
        return copy

    grads[0, chan] = shard_ref[...]
    empty = jnp.zeros((6, 32, 128), BF16)
    acts[:, 0] = empty
    acts[:, 5] = empty
    acts[1:5, 1:5] = act_ref[...]
    acc[...] = jnp.zeros(acc.shape, F32)
    pl.semaphore_wait(barrier, len(partners))

    own = [
        remote(shard_ref, grads.at[0, chan], s_own.at[d - 1], r_own.at[d - 1], {"chan": (chan + d) % nc})
        for d in range(1, nc)
    ]
    up = remote(act_ref.at[3], acts.at[0, pl.ds(1, 4)], s_act.at[0], r_act.at[0], {"space": after})
    down = remote(act_ref.at[0], acts.at[5, pl.ds(1, 4)], s_act.at[1], r_act.at[1], {"space": before})
    over = {}
    for d in range(1, nf):
        over[d] = remote(
            shard_ref, grads.at[d, chan], s_filt.at[d - 1], r_filt.at[d - 1], {"filt": (filt + d) % nf}
        )
    wover = {}
    for d in range(1, nf):
        target = (filt + d) % nf
        wover[d] = remote(
            taps_ref.at[target, pl.ds(pl.multiple_of(row * w_rows, w_rows), w_rows)],
            wparts.at[row, d - 1], s_wf.at[d - 1], r_wf.at[d - 1], {"filt": target},
        )

    rim = jnp.zeros((6, 256, 128), F32)
    for x in (0, 1, 6, 7):
        prod[x] = rim
    for x in range(2, 6):
        prod[x, 0] = rim[0]
        prod[x, 5] = rim[0]

    lane = lax.broadcasted_iota(jnp.int32, (1, 128), 1)
    first, last = lane == 0, lane == 127

    for copy in own:
        copy.wait_recv()
    up.wait_recv()
    down.wait_recv()
    zero = jnp.zeros((4, 32, 128), BF16)
    acts[0, 1:5] = jnp.where(space > 0, acts[0, 1:5], zero)
    acts[5, 1:5] = jnp.where(space < ns - 1, acts[5, 1:5], zero)

    def pair_of(block):
        parts = block.astype(F32).reshape(-1, 2, own_filt, 128)
        return [parts[:, i].reshape(-1, 128) for i in range(2)]

    def taps_step(h, carry):
        x, z = h // 2, (h % 2) * 2
        start = pl.multiple_of(h * 2 * own_filt, 2 * own_filt)
        columns = []
        for g in pair_of(grads[0, :, pl.ds(start, 2 * own_filt), :]):
            low = jnp.where(last, 0.0, pltpu.roll(g, 127, 1))
            high = jnp.where(first, 0.0, pltpu.roll(g, 1, 1))
            columns.append(jnp.concatenate([low, g, high], axis=0).astype(BF16))
        rhs = jnp.concatenate(columns, axis=1)
        halves = [
            jnp.concatenate([acts[x + a, z + c + i] for a in range(3) for c in range(3)], axis=0)
            for i in range(2)
        ]
        acc[:, 0:192] += lax.dot_general(
            jnp.concatenate(halves, axis=1), rhs, (((1,), (1,)), ((), ())), preferred_element_type=F32
        )
        return carry

    lax.fori_loop(0, 8, taps_step, 0)
    mine[0:288] = acc[:, 0:128] * scale
    third = acc[:, 128:256] * scale
    mine[288:432] = jnp.where(lane < 64, third[0:144], pltpu.roll(third[144:288], 64, 1))
    mine[432:512] = jnp.zeros((80, 128), F32)

    y_red = []
    for d in range(1, ny):
        theirs = pl.multiple_of((row + d) % ny * y_rows, y_rows)
        y_red.append(
            remote(mine.at[pl.ds(theirs, y_rows)], from_y.at[d - 1], s_yr.at[d - 1], r_yr.at[d - 1], at_y(d))
        )

    x_copies, sib_copies = {}, {}

    def forward(d):
        over[d].wait_recv()
        for e in range(1, nx):
            x_copies[d, e] = remote(
                grads.at[d, chan], grads.at[d, chan], s_x.at[d - 1, e - 1], r_x.at[d - 1, e - 1], at_x(e)
            )
        sib_copies[d, 0] = remote(
            grads.at[d, chan], grads.at[d, chan], s_sib.at[d - 1, 0], r_sib.at[d - 1, 0], {"chan": sib}
        )

    def share(d):
        for e in range(1, nx):
            x_copies[d, e].wait_recv()
            source = ((chip + nx - e) % nx) * 2 + core
            sib_copies[d, e] = remote(
                grads.at[d, source], grads.at[d, source], s_sib.at[d - 1, e], r_sib.at[d - 1, e], {"chan": sib}
            )

    forward(1)
    forward(3)

    mine_y = pl.multiple_of(row * y_rows, y_rows)
    for copy in y_red:
        copy.wait_recv()
    part = mine[pl.ds(mine_y, y_rows)]
    for d in range(1, ny):
        part = part + from_y[d - 1]
    for_z[...] = part
    z_red = []
    for d in range(1, nz):
        theirs = pl.multiple_of((run + d) % nz * z_rows, z_rows)
        z_red.append(
            remote(for_z.at[pl.ds(theirs, z_rows)], from_z.at[d - 1], s_zr.at[d - 1], r_zr.at[d - 1], at_z(d))
        )

    for d in range(1, nf):
        wover[d].wait_recv()
    wshare = [
        remote(wparts.at[row], wparts.at[row], s_wy.at[d - 1], r_wy.at[d - 1], at_y(d)) for d in range(1, ny)
    ]
    forward(2)
    share(1)
    share(3)

    for copy in z_red:
        copy.wait_recv()
    part = for_z[pl.ds(pl.multiple_of(run * z_rows, z_rows), z_rows)]
    for d in range(1, nz):
        part = part + from_z[d - 1]
    place = pl.ds(pl.multiple_of(mine_y + run * z_rows, z_rows), z_rows)
    total[place] = part
    z_gat = [
        remote(total.at[place], total.at[place], s_zg.at[d - 1], r_zg.at[d - 1], at_z(d)) for d in range(1, nz)
    ]
    share(2)

    for copy in wshare:
        copy.wait_recv()
    blocks = [taps_ref[filt].astype(F32)]
    blocks += [wparts[:, d].reshape(TAP_ROWS, 128).astype(F32) for d in range(nf - 1)]
    for i in range(0, nf, 2):
        a, b = blocks[i], blocks[i + 1]
        lhs[0:128, i * 64 : i * 64 + 128] = jnp.where(lane < 64, a, pltpu.roll(b, 64, 1)).astype(BF16)
        lhs[128:256, i * 64 : i * 64 + 128] = jnp.where(lane < 64, pltpu.roll(a, 64, 1), b).astype(BF16)

    for copy in z_gat:
        copy.wait_recv()
    place_y = pl.ds(mine_y, y_rows)
    y_gat = [
        remote(total.at[place_y], total.at[place_y], s_yg.at[d - 1], r_yg.at[d - 1], at_y(d)) for d in range(1, ny)
    ]

    for copy in sib_copies.values():
        copy.wait_recv()

    def prod_step(h, carry):
        x, z = h // 2, (h % 2) * 2
        start = pl.multiple_of(h * 2 * own_filt, 2 * own_filt)
        block = grads[:, :, pl.ds(start, 2 * own_filt), :].reshape(nf * nc, 2 * own_filt, 128)
        rhs = jnp.concatenate(pair_of(block), axis=1).astype(BF16)
        result = jnp.dot(lhs[...], rhs, preferred_element_type=F32)
        prod[x + 2, z + 1] = result[:, :128]
        prod[x + 2, z + 2] = result[:, 128:]
        return carry

    lax.fori_loop(0, 8, prod_step, 0)

    def sum_step(n, x):
        z = n
        sums = []
        for b in range(3):
            terms = []
            for a in range(3):
                for c in range(3):
                    k = (a * 3 + b) * 3 + c
                    at = (k % 2) * 128 + (k // 2) * 8
                    terms.append(prod[x + 2 - a, z + 2 - c, at : at + 8])
            sums.append(functools.reduce(jnp.add, terms))
        low = jnp.where(last, 0.0, pltpu.roll(sums[0], 127, 1))
        high = jnp.where(first, 0.0, pltpu.roll(sums[2], 1, 1))
        outs[x, z] = sums[1] + low + high
        return x

    def layer(x):
        for n in range(4):
            sum_step(n, x)

    layer(0)
    low_out = remote(outs.at[0], halo.at[1], s_halo.at[0], r_halo.at[0], {"space": before})
    layer(5)
    high_out = remote(outs.at[5], halo.at[0], s_halo.at[1], r_halo.at[1], {"space": after})

    def inner(x, carry):
        layer(x)
        return carry

    lax.fori_loop(1, 5, inner, 0)

    for copy in y_gat:
        copy.wait_recv()
    for a in range(3):
        for c in range(3):
            block = (a * 3 + c) * 32
            for b in range(2):
                gw_ref[(a * 3 + b) * 3 + c] = total[block : block + 32, b * 64 : b * 64 + 64]
            for half in range(2):
                at = block + half * 16
                left = 0 if at < 144 else 64
                src = 288 + (at if at < 144 else at - 144)
                gw_ref[(a * 3 + 2) * 3 + c, half * 16 : half * 16 + 16] = total[src : src + 16, left : left + 64]

    low_out.wait_recv()
    high_out.wait_recv()
    outs[1] = outs[1] + jnp.where(space > 0, halo[0], 0.0)
    outs[4] = outs[4] + jnp.where(space < ns - 1, halo[1], 0.0)
    gi_ref[...] = outs[1:5].reshape(128, 128).astype(BF16)
    for copy in sent:
        copy.wait_send()


def body(sizes, activations, out_grad, weight):
    ny, nz, nx, nf = sizes
    nc = nx * 2
    act = jnp.transpose(activations, (1, 2, 0, 3))
    own_filt = out_grad.shape[1]
    shard = jnp.transpose(out_grad[0], (1, 2, 0, 3)).reshape(16 * own_filt, 128)
    taps = jnp.pad(weight, ((0, 5), (0, 0), (0, 0))).reshape(16, 2, nf, 8, 64)
    taps = jnp.transpose(taps, (2, 0, 3, 1, 4)).reshape(nf, TAP_ROWS, 128)
    cells = 16 * 128 * ny * nz
    dma = pltpu.SemaphoreType.DMA
    vmem = pl.BlockSpec(memory_space=pltpu.VMEM)
    y_rows = ROWS // ny
    z_rows = y_rows // nz
    pairs = []
    for shape in (
        (nc - 1,), (2,), (nf - 1,), (nf - 1,), (ny - 1,), (nf - 1, max(nx - 1, 1)), (nf - 1, nx),
        (ny - 1,), (nz - 1,), (nz - 1,), (ny - 1,), (2,),
    ):
        pairs += [dma(shape), dma(shape)]
    gi, gw = pl.pallas_call(
        functools.partial(kernel, sizes, 1.0 / math.sqrt(cells)),
        out_shape=(
            jax.ShapeDtypeStruct((128, 128), BF16),
            jax.ShapeDtypeStruct((27, 32, 64), F32),
        ),
        in_specs=[vmem] * 3,
        out_specs=(vmem, vmem),
        scratch_shapes=[
            pltpu.VMEM((nf, nc, 16 * own_filt, 128), BF16),
            pltpu.VMEM((6, 6, 32, 128), BF16),
            pltpu.VMEM((ny, nf - 1, TAP_ROWS // ny, 128), BF16),
            pltpu.VMEM((256, 256), BF16),
            pltpu.VMEM((288, 256), F32),
            pltpu.VMEM((ROWS, 128), F32),
            pltpu.VMEM((ny - 1, y_rows, 128), F32),
            pltpu.VMEM((y_rows, 128), F32),
            pltpu.VMEM((nz - 1, z_rows, 128), F32),
            pltpu.VMEM((ROWS, 128), F32),
            pltpu.VMEM((8, 6, 256, 128), F32),
            pltpu.VMEM((6, 4, 8, 128), F32),
            pltpu.VMEM((2, 4, 8, 128), F32),
        ] + pairs,
        compiler_params=pltpu.CompilerParams(
            collective_id=0, has_side_effects=True, vmem_limit_bytes=32 * 1024 * 1024
        ),
    )(act, shard, taps)
    return jnp.transpose(gi.reshape(4, 4, 8, 128), (2, 0, 1, 3)), gw


def solution(mesh):
    ns = mesh.shape["space"]
    nz = 8 if ns % 8 == 0 else 2
    sizes = (ns // nz, nz, mesh.shape["chan"] // 2, mesh.shape["filt"])
    return jax.shard_map(
        functools.partial(body, sizes),
        mesh=mesh,
        in_specs=(
            P("chan", "space", None, None),
            P("filt", "chan", "space", None, None),
            P(None, "chan", "filt"),
        ),
        out_specs=(P(("chan", "filt"), "space", None, None), P(None, "chan", "filt")),
        check_vma=False,
    )
```

time: 538 us -> 75.5 us (0.14)
  waiting for transfers between devices: 325 us -> 0 us
  blocking collectives: 84.1 us -> 0 us
  local copies, waits for them, and re-layouts: 84.1 us -> 3.54 us
  Pallas kernels: 0 us -> 70.4 us
  matrix products: 24.5 us -> 0 us
  between operations: 15.1 us -> 0.68 us
    psum x1 -> x0, waiting for transfers between devices: 322 us -> none  [body(): grad_weight = lax.psum(local_taps, 'space')]
    pallas_call x0 -> x1, Pallas kernels: none -> 70.4 us  [body(): pl.pallas_call(functools.partial(kernel, sizes, 1.0 / math.sqrt(cells)),...]
    unnamed x1 -> x0, blocking collectives: 62.8 us -> none
    reshape x28 -> x3, local copies, waits for them, and re-layouts: 37.7 us -> 0.98 us  [the longest x1 0.63 us: body(): return (jnp.transpose(gi.reshape(4, 4, 8, 128), (2, 0, 1, 3)), gw)]
    slice x30 -> x0, local copies, waits for them, and re-layouts: 33.8 us -> none  [the longest x29 33.8 us: body(): padded[:, 2 - shift_x:2 - shift_x + count_x, 2 - shift_z:2 - shift_z + co...]
    dot_general x54 -> x0, matrix products: 24.5 us -> none  [the longest x27 17.7 us: body(): jnp.dot(weight[tap_index], shifted, preferred_element_type=jnp.float32)]
    all_gather x1 -> x0, blocking collectives: 21.4 us -> none  [body(): grad_full = lax.all_gather(out_grad, 'chan', axis=1, tiled=True)]
    unnamed x47 -> x4, local copies, waits for them, and re-layouts: 12 us -> 1.71 us
  transfers between devices with their start and end apart: 3 -> 0, of which waited for: 2 -> 0; matrix products, arithmetic and copies ran while one was open for 16% -> 0% of each run, Pallas kernels for 0% -> 0%
where the time goes in v1:
time: 75.5 us; the launch traced here: 74.6 us
  Pallas kernels  70.4 us (93%)
  local copies, waits for them, and re-layouts  3.54 us (5%)
    pallas_call x1, Pallas kernels, body(): pl.pallas_call(functools.partial(kernel, sizes, 1.0 / math.sqrt(cells)),...  70.4 us
    unnamed x4, local copies, waits for them, and re-layouts  1.71 us

profile of v1, /device:TPU:6, one launch (start us, length us, event | category | flops | bytes accessed | tf_op | source)
XLA Modules:
  0.0 74.6 jit_solution(6867412179240854148)
XLA Ops:
  0.6 0.0 copy-start
  0.6 0.8 %copy.6 = bf16[4,4,8,128]{3,2,1,0:T(8,128)(2,1)S(1)} copy(bf16[4,4,8,128]{3,1,0,2:T(4,128)(2,1)} %bitcast.20) | data formatting | bytes 65536 | tf_op jit(solution)/shard_map/transpose | solution.py:292
  1.5 0.9 %copy.13 = bf16[32,4,4,128]{3,0,2,1:T(8,128)(2,1)S(1)} copy(bf16[32,4,4,128]{3,2,1,0:T(4,128)(2,1)} %param.3) | data formatting | bytes 262144 | tf_op args[0]
  2.4 0.0 copy-done
  2.5 0.2 copy.12
  2.7 0.1 reshape.18.taps_ref
  2.8 70.4 %shard_map.50 = (bf16[128,128]{1,0:T(8,128)(2,1)S(1)}, f32[27,32,64]{2,1,0:T(8,128)S(1)}) custom-call(bf16[4,4,32,128]{3,2,1,0:T(8,128)(2,1)S(1)} %bitcast.15, bf16[128,128]{1,0:T(8,128)(2,1)S(1)} %bitcast.16, bf16[4,128,128]{2,1,0:T(8,128)(2,1)S(1)} %reshape.18.taps_ref), custom_call_target="tpu_custom_call" | custom-call | tf_op jit(solution)/shard_map/pallas_call | solution.py:306
  73.2 0.6 copy.14
  73.8 0.8 %copy.16 = f32[27,32,64]{2,1,0:T(8,128)} copy(f32[27,32,64]{2,1,0:T(8,128)S(1)} %get-tuple-element.9) | data formatting | bytes 442368
  (1 shorter events, 0.0 us)
Async XLA Ops:
  0.6 1.8 %copy-start = (bf16[27,32,64]{2,1,0:T(8,128)(2,1)S(1)}, bf16[27,32,64]{2,1,0:T(8,128)(2,1)}, u32[]{:S(2)}) copy-start(bf16[27,32,64]{2,1,0:T(8,128)(2,1)} %param.5) | copy-start | bytes 331780

commit v2 on v1

--- a/solution.py
+++ b/solution.py
@@ -16,8 +16,9 @@
 
 def kernel(
     sizes, scale,
-    act_ref, shard_ref, taps_ref,
+    act_hbm, shard_hbm, weight_hbm,
     gi_ref, gw_ref,
+    act_raw, shard_raw, weight_raw, act_stage, shard_stage, shard_ref, taps_ref, in_sems, told,
     grads, acts, wparts, lhs, acc, mine, from_y, for_z, from_z, total, prod, outs, halo,
     s_own, r_own, s_act, r_act, s_filt, r_filt, s_wf, r_wf, s_wy, r_wy, s_x, r_x, s_sib, r_sib,
     s_yr, r_yr, s_zr, r_zr, s_zg, r_zg, s_yg, r_yg, s_halo, r_halo,
@@ -44,50 +45,108 @@
     def at_x(d):
         return {"chan": ((chip + d) % nx) * 2 + core}
 
+    rank = jnp.where(filt < 2, filt, 5 - filt)
+
+    def filt_at(d):
+        target = (filt + d) % nf
+        return target, jnp.where(target < 2, target, 5 - target)
+
     barrier = pltpu.get_barrier_semaphore()
     partners = [{"chan": (chan + d) % nc} for d in range(1, nc)]
-    partners += [{"filt": (filt + d) % nf} for d in range(1, nf)]
     partners += [at_y(d) for d in range(1, ny)] + [at_z(d) for d in range(1, nz)]
     partners += [{"space": before}, {"space": after}]
     for partner in partners:
         pl.semaphore_signal(barrier, inc=1, device_id=partner, device_id_type=MESH)
+    for d in range(1, nf):
+        target, target_rank = filt_at(d)
+
+        @pl.when(rank < target_rank)
+        def _(target=target):
+            pl.semaphore_signal(barrier, inc=1, device_id={"filt": target}, device_id_type=MESH)
+
+    loads = [
+        pltpu.make_async_copy(src, dst, in_sems.at[n])
+        for n, (src, dst) in enumerate(((shard_hbm, shard_raw), (act_hbm, act_raw), (weight_hbm, weight_raw)))
+    ]
+    for load in loads:
+        load.start()
 
     sent = []
 
-    def remote(src, dst, ssem, rsem, where):
+    def remote(src, dst, ssem, rsem, where, start=True):
         copy = pltpu.make_async_remote_copy(
             src_ref=src, dst_ref=dst, send_sem=ssem, recv_sem=rsem, device_id=where, device_id_type=MESH
         )
-        copy.start()
+        if start:
+            copy.start()
         sent.append(copy)
         return copy
 
+    lane = lax.broadcasted_iota(jnp.int32, (1, 128), 1)
+    first, last = lane == 0, lane == 127
+    loads[0].wait()
+    for o in range(own_filt):
+        shard_stage[:, :, o, :] = shard_raw[0, o].astype(F32)
+    shard_ref[...] = shard_stage[...].reshape(shard_rows, 128).astype(BF16)
     grads[0, chan] = shard_ref[...]
+    loads[1].wait()
+    for i in range(32):
+        act_stage[:, :, i, :] = act_raw[i].astype(F32)
+    acts[1:5, 1:5] = act_stage[...].astype(BF16)
     empty = jnp.zeros((6, 32, 128), BF16)
     acts[:, 0] = empty
     acts[:, 5] = empty
-    acts[1:5, 1:5] = act_ref[...]
+    loads[2].wait()
+    blank = jnp.zeros((8, 64), F32)
+    for block in range(nf):
+        pieces = []
+        for k in range(0, 32, 2):
+            pair = [
+                weight_raw[t].astype(F32)[block * 8 : block * 8 + 8] if t < 27 else blank for t in (k, k + 1)
+            ]
+            pieces.append(jnp.concatenate(pair, axis=1))
+        taps_ref[block] = jnp.concatenate(pieces, axis=0).astype(BF16)
     acc[...] = jnp.zeros(acc.shape, F32)
-    pl.semaphore_wait(barrier, len(partners))
-
+    pl.semaphore_wait(barrier, len(partners) + rank)
+
+    over, wover = {}, {}
+    for d in range(1, nf):
+        target, target_rank = filt_at(d)
+        over[d] = remote(
+            shard_ref, grads.at[d, chan], s_filt.at[d - 1], r_filt.at[d - 1], {"filt": target}, start=False
+        )
+        wover[d] = remote(
+            taps_ref.at[target, pl.ds(pl.multiple_of(row * w_rows, w_rows), w_rows)],
+            wparts.at[row, d - 1], s_wf.at[d - 1], r_wf.at[d - 1], {"filt": target}, start=False,
+        )
+
+    def send_back(d):
+        target, target_rank = filt_at(d)
+
+        @pl.when(rank > target_rank)
+        def _():
+            pl.semaphore_signal(told.at[d - 1], inc=1, device_id={"filt": target}, device_id_type=MESH)
+            over[d].start()
+            wover[d].start()
+
+    def send_on(d, who):
+        target, target_rank = filt_at(d)
+
+        @pl.when(functools.reduce(jnp.logical_or, [filt == w for w in who]))
+        def _():
+            pl.semaphore_wait(told.at[nf - d - 1], 1)
+            over[d].start()
+            wover[d].start()
+
+    send_back(2)
+    send_back(1)
+    send_back(3)
     own = [
         remote(shard_ref, grads.at[0, chan], s_own.at[d - 1], r_own.at[d - 1], {"chan": (chan + d) % nc})
         for d in range(1, nc)
     ]
-    up = remote(act_ref.at[3], acts.at[0, pl.ds(1, 4)], s_act.at[0], r_act.at[0], {"space": after})
-    down = remote(act_ref.at[0], acts.at[5, pl.ds(1, 4)], s_act.at[1], r_act.at[1], {"space": before})
-    over = {}
-    for d in range(1, nf):
-        over[d] = remote(
-            shard_ref, grads.at[d, chan], s_filt.at[d - 1], r_filt.at[d - 1], {"filt": (filt + d) % nf}
-        )
-    wover = {}
-    for d in range(1, nf):
-        target = (filt + d) % nf
-        wover[d] = remote(
-            taps_ref.at[target, pl.ds(pl.multiple_of(row * w_rows, w_rows), w_rows)],
-            wparts.at[row, d - 1], s_wf.at[d - 1], r_wf.at[d - 1], {"filt": target},
-        )
+    up = remote(acts.at[4, pl.ds(1, 4)], acts.at[0, pl.ds(1, 4)], s_act.at[0], r_act.at[0], {"space": after})
+    down = remote(acts.at[1, pl.ds(1, 4)], acts.at[5, pl.ds(1, 4)], s_act.at[1], r_act.at[1], {"space": before})
 
     rim = jnp.zeros((6, 256, 128), F32)
     for x in (0, 1, 6, 7):
@@ -95,9 +154,6 @@
     for x in range(2, 6):
         prod[x, 0] = rim[0]
         prod[x, 5] = rim[0]
-
-    lane = lax.broadcasted_iota(jnp.int32, (1, 128), 1)
-    first, last = lane == 0, lane == 127
 
     for copy in own:
         copy.wait_recv()
@@ -162,8 +218,9 @@
                 grads.at[d, source], grads.at[d, source], s_sib.at[d - 1, e], r_sib.at[d - 1, e], {"chan": sib}
             )
 
-    forward(1)
-    forward(3)
+    send_on(1, (1,))
+    send_on(3, (3,))
+    send_on(2, (1,))
 
     mine_y = pl.multiple_of(row * y_rows, y_rows)
     for copy in y_red:
@@ -179,14 +236,10 @@
             remote(for_z.at[pl.ds(theirs, z_rows)], from_z.at[d - 1], s_zr.at[d - 1], r_zr.at[d - 1], at_z(d))
         )
 
-    for d in range(1, nf):
-        wover[d].wait_recv()
-    wshare = [
-        remote(wparts.at[row], wparts.at[row], s_wy.at[d - 1], r_wy.at[d - 1], at_y(d)) for d in range(1, ny)
-    ]
-    forward(2)
-    share(1)
-    share(3)
+    send_on(1, (0,))
+    send_on(3, (0,))
+    forward(1)
+    forward(3)
 
     for copy in z_red:
         copy.wait_recv()
@@ -198,17 +251,26 @@
     z_gat = [
         remote(total.at[place], total.at[place], s_zg.at[d - 1], r_zg.at[d - 1], at_z(d)) for d in range(1, nz)
     ]
-    share(2)
+    send_on(2, (0,))
+    share(1)
+    share(3)
+    for d in range(1, nf):
+        wover[d].wait_recv()
+    wshare = [
+        remote(wparts.at[row], wparts.at[row], s_wy.at[d - 1], r_wy.at[d - 1], at_y(d)) for d in range(1, ny)
+    ]
+    forward(2)
 
     for copy in wshare:
         copy.wait_recv()
     blocks = [taps_ref[filt].astype(F32)]
-    blocks += [wparts[:, d].reshape(TAP_ROWS, 128).astype(F32) for d in range(nf - 1)]
+    blocks += [wparts[:, d].reshape(TAP_ROWS, 128).astype(F32) for d in (0, 2, 1)]
     for i in range(0, nf, 2):
         a, b = blocks[i], blocks[i + 1]
         lhs[0:128, i * 64 : i * 64 + 128] = jnp.where(lane < 64, a, pltpu.roll(b, 64, 1)).astype(BF16)
         lhs[128:256, i * 64 : i * 64 + 128] = jnp.where(lane < 64, pltpu.roll(a, 64, 1), b).astype(BF16)
 
+    share(2)
     for copy in z_gat:
         copy.wait_recv()
     place_y = pl.ds(mine_y, y_rows)
@@ -216,20 +278,30 @@
         remote(total.at[place_y], total.at[place_y], s_yg.at[d - 1], r_yg.at[d - 1], at_y(d)) for d in range(1, ny)
     ]
 
-    for copy in sib_copies.values():
-        copy.wait_recv()
-
-    def prod_step(h, carry):
-        x, z = h // 2, (h % 2) * 2
-        start = pl.multiple_of(h * 2 * own_filt, 2 * own_filt)
-        block = grads[:, :, pl.ds(start, 2 * own_filt), :].reshape(nf * nc, 2 * own_filt, 128)
-        rhs = jnp.concatenate(pair_of(block), axis=1).astype(BF16)
-        result = jnp.dot(lhs[...], rhs, preferred_element_type=F32)
-        prod[x + 2, z + 1] = result[:, :128]
-        prod[x + 2, z + 2] = result[:, 128:]
-        return carry
-
-    lax.fori_loop(0, 8, prod_step, 0)
+    def product(which, columns, add):
+        def step(h, carry):
+            x, z = h // 2, (h % 2) * 2
+            start = pl.multiple_of(h * 2 * own_filt, 2 * own_filt)
+            parts = [pair_of(grads[d, :, pl.ds(start, 2 * own_filt), :]) for d in which]
+            rhs = jnp.concatenate(
+                [jnp.concatenate([p[i] for p in parts], axis=0) for i in range(2)], axis=1
+            ).astype(BF16)
+            result = jnp.dot(lhs[:, columns], rhs, preferred_element_type=F32)
+            for i in range(2):
+                half = result[:, i * 128 : i * 128 + 128]
+                prod[x + 2, z + 1 + i] = prod[x + 2, z + 1 + i] + half if add else half
+            return carry
+
+        lax.fori_loop(0, 8, step, 0)
+
+    for (d, e), copy in sib_copies.items():
+        if d != 2:
+            copy.wait_recv()
+    product((0, 1, 3), slice(0, 192), False)
+    for (d, e), copy in sib_copies.items():
+        if d == 2:
+            copy.wait_recv()
+    product((2,), slice(192, 256), True)
 
     def sum_step(n, x):
         z = n
@@ -287,14 +359,11 @@
 def body(sizes, activations, out_grad, weight):
     ny, nz, nx, nf = sizes
     nc = nx * 2
-    act = jnp.transpose(activations, (1, 2, 0, 3))
     own_filt = out_grad.shape[1]
-    shard = jnp.transpose(out_grad[0], (1, 2, 0, 3)).reshape(16 * own_filt, 128)
-    taps = jnp.pad(weight, ((0, 5), (0, 0), (0, 0))).reshape(16, 2, nf, 8, 64)
-    taps = jnp.transpose(taps, (2, 0, 3, 1, 4)).reshape(nf, TAP_ROWS, 128)
     cells = 16 * 128 * ny * nz
     dma = pltpu.SemaphoreType.DMA
     vmem = pl.BlockSpec(memory_space=pltpu.VMEM)
+    hbm = pl.BlockSpec(memory_space=pl.ANY)
     y_rows = ROWS // ny
     z_rows = y_rows // nz
     pairs = []
@@ -309,9 +378,18 @@
             jax.ShapeDtypeStruct((128, 128), BF16),
             jax.ShapeDtypeStruct((27, 32, 64), F32),
         ),
-        in_specs=[vmem] * 3,
+        in_specs=[hbm] * 3,
         out_specs=(vmem, vmem),
         scratch_shapes=[
+            pltpu.VMEM(activations.shape, BF16),
+            pltpu.VMEM(out_grad.shape, BF16),
+            pltpu.VMEM(weight.shape, BF16),
+            pltpu.VMEM((4, 4, 32, 128), F32),
+            pltpu.VMEM((4, 4, own_filt, 128), F32),
+            pltpu.VMEM((16 * own_filt, 128), BF16),
+            pltpu.VMEM((nf, TAP_ROWS, 128), BF16),
+            dma((3,)),
+            pltpu.SemaphoreType.REGULAR((nf - 1,)),
             pltpu.VMEM((nf, nc, 16 * own_filt, 128), BF16),
             pltpu.VMEM((6, 6, 32, 128), BF16),
             pltpu.VMEM((ny, nf - 1, TAP_ROWS // ny, 128), BF16),
@@ -329,7 +407,7 @@
         compiler_params=pltpu.CompilerParams(
             collective_id=0, has_side_effects=True, vmem_limit_bytes=32 * 1024 * 1024
         ),
-    )(act, shard, taps)
+    )(activations, out_grad, weight)
     return jnp.transpose(gi.reshape(4, 4, 8, 128), (2, 0, 1, 3)), gw
 
 

time: 75.5 us -> 69.4 us (0.919)
  the two profiles are of different devices: /device:TPU:6 before, /device:TPU:1 now
where the time goes in v2:
time: 69.4 us; the launch traced here: 69.1 us
  Pallas kernels  64.5 us (93%)
  local copies, waits for them, and re-layouts  3.98 us (6%)
    pallas_call x1, Pallas kernels, body(): pl.pallas_call(functools.partial(kernel, sizes, 1.0 / math.sqrt(cells)),...  64.5 us
    unnamed x7, local copies, waits for them, and re-layouts  3.35 us

profile of v2, /device:TPU:1, one launch (start us, length us, event | category | flops | bytes accessed | tf_op | source)
XLA Modules:
  0.0 69.1 jit_solution(10686519111060362287)
XLA Ops:
  0.6 0.0 copy-start
  0.6 0.9 %copy-done = bf16[27,32,64]{2,1,0:T(8,128)(2,1)S(1)} copy-done((bf16[27,32,64]{2,1,0:T(8,128)(2,1)S(1)}, bf16[27,32,64]{2,1,0:T(8,128)(2,1)}, u32[]{:S(2)}) %copy-start) | copy-done | bytes 110616
  1.6 0.0 copy-start.1
  1.6 0.9 %copy-done.1 = bf16[32,4,4,128]{3,2,1,0:T(4,128)(2,1)S(1)} copy-done((bf16[32,4,4,128]{3,2,1,0:T(4,128)(2,1)S(1)}, bf16[32,4,4,128]{3,2,1,0:T(4,128)(2,1)}, u32[]{:S(2)}) %copy-start.1) | copy-done | bytes 131096
  2.5 0.0 copy-start.2
  2.5 0.8 %copy-done.2 = bf16[1,8,4,4,128]{4,3,2,1,0:T(4,128)(2,1)S(1)} copy-done((bf16[1,8,4,4,128]{4,3,2,1,0:T(4,128)(2,1)S(1)}, bf16[1,8,4,4,128]{4,3,2,1,0:T(4,128)(2,1)}, u32[]{:S(2)}) %copy-start.2) | copy-done | bytes 32792
  3.2 64.5 %shard_map.50 = (bf16[128,128]{1,0:T(8,128)(2,1)S(1)}, f32[27,32,64]{2,1,0:T(8,128)S(1)}) custom-call(bf16[32,4,4,128]{3,2,1,0:T(4,128)(2,1)S(1)} %copy-done.1, bf16[1,8,4,4,128]{4,3,2,1,0:T(4,128)(2,1)S(1)} %copy-done.2, bf16[27,32,64]{2,1,0:T(8,128)(2,1)S(1)} %copy-done), custom_call_target="tpu_custom_call" | custom-call | tf_op jit(solution)/shard_map/pallas_call | solution.py:375
  67.7 0.6 copy.7
  68.3 0.8 %copy.9 = f32[27,32,64]{2,1,0:T(8,128)} copy(f32[27,32,64]{2,1,0:T(8,128)S(1)} %get-tuple-element.9) | data formatting | bytes 442368
Async XLA Ops:
  0.6 0.9 %copy-start = (bf16[27,32,64]{2,1,0:T(8,128)(2,1)S(1)}, bf16[27,32,64]{2,1,0:T(8,128)(2,1)}, u32[]{:S(2)}) copy-start(bf16[27,32,64]{2,1,0:T(8,128)(2,1)} %weight_hbm.1) | copy-start | bytes 331780
  1.6 0.9 %copy-start.1 = (bf16[32,4,4,128]{3,2,1,0:T(4,128)(2,1)S(1)}, bf16[32,4,4,128]{3,2,1,0:T(4,128)(2,1)}, u32[]{:S(2)}) copy-start(bf16[32,4,4,128]{3,2,1,0:T(4,128)(2,1)} %act_hbm.1) | copy-start | bytes 393220
  2.5 0.8 %copy-start.2 = (bf16[1,8,4,4,128]{4,3,2,1,0:T(4,128)(2,1)S(1)}, bf16[1,8,4,4,128]{4,3,2,1,0:T(4,128)(2,1)}, u32[]{:S(2)}) copy-start(bf16[1,8,4,4,128]{4,3,2,1,0:T(4,128)(2,1)} %shard_hbm.1) | copy-start | bytes 98308

commit v3 on v2

--- a/solution.py
+++ b/solution.py
@@ -19,8 +19,8 @@
     act_hbm, shard_hbm, weight_hbm,
     gi_ref, gw_ref,
     act_raw, shard_raw, weight_raw, act_stage, shard_stage, shard_ref, taps_ref, in_sems, told,
-    grads, acts, wparts, lhs, acc, mine, from_y, for_z, from_z, total, prod, outs, halo,
-    s_own, r_own, s_act, r_act, s_filt, r_filt, s_wf, r_wf, s_wy, r_wy, s_x, r_x, s_sib, r_sib,
+    grads, acts, wparts, lhs, late, acc, mine, from_y, for_z, from_z, total, prod, outs, halo,
+    s_own, r_own, s_act, r_act, s_filt, r_filt, s_wf, r_wf, s_wy, r_wy, s_pass, r_pass, s_edge, r_edge, s_pe, r_pe,
     s_yr, r_yr, s_zr, r_zr, s_zg, r_zg, s_yg, r_yg, s_halo, r_halo,
 ):
     ny, nz, nx, nf = sizes
@@ -28,13 +28,24 @@
     space, chan, filt = lax.axis_index("space"), lax.axis_index("chan"), lax.axis_index("filt")
     row, run = space // nz, space % nz
     chip, core = chan // 2, chan % 2
-    sib = chip * 2 + (1 - core)
     shard_rows = shard_ref.shape[0]
     own_filt = shard_rows // 16
     y_rows = ROWS // ny
     z_rows = y_rows // nz
-    w_rows = TAP_ROWS // ny
+    w_rows = TAP_ROWS // (2 * ny)
+    layer_rows = 4 * own_filt
+    inner_rows = pl.ds(layer_rows, 4 * layer_rows)
+    w_mine = row * 2 + run % 2
     before, after = (space + ns - 1) % ns, (space + 1) % ns
+    at_low, at_high = run == 0, run == nz - 1
+    at_end = jnp.logical_or(at_low, at_high)
+    across = jnp.where(at_low, before, after)
+    edge_from = jnp.where(at_low, 0, 3)
+    edge_to = jnp.where(at_low, 5, 0)
+    edge_in = jnp.where(at_low, 0, 5)
+
+    def layers(x):
+        return pl.ds(pl.multiple_of(x * layer_rows, layer_rows), layer_rows)
 
     def at_y(d):
         return {"space": ((row + d) % ny) * nz + run}
@@ -42,27 +53,31 @@
     def at_z(d):
         return {"space": row * nz + (run + d) % nz}
 
-    def at_x(d):
-        return {"chan": ((chip + d) % nx) * 2 + core}
-
-    rank = jnp.where(filt < 2, filt, 5 - filt)
+    def at_w(e):
+        return {"space": (row + e // 2) % ny * nz + (run + e % 2 - 2 * (e % 2) * (run % 2))}
+
 
     def filt_at(d):
-        target = (filt + d) % nf
-        return target, jnp.where(target < 2, target, 5 - target)
+        return (filt + d) % nf
 
     barrier = pltpu.get_barrier_semaphore()
     partners = [{"chan": (chan + d) % nc} for d in range(1, nc)]
     partners += [at_y(d) for d in range(1, ny)] + [at_z(d) for d in range(1, nz)]
     partners += [{"space": before}, {"space": after}]
+    partners += [at_w(2 * e + 1) for e in range(1, ny)]
     for partner in partners:
         pl.semaphore_signal(barrier, inc=1, device_id=partner, device_id_type=MESH)
     for d in range(1, nf):
-        target, target_rank = filt_at(d)
-
-        @pl.when(rank < target_rank)
+        target = filt_at(d)
+
+        @pl.when(filt < target)
         def _(target=target):
             pl.semaphore_signal(barrier, inc=1, device_id={"filt": target}, device_id_type=MESH)
+
+            @pl.when(at_end)
+            def _():
+                where = {"filt": target, "space": across}
+                pl.semaphore_signal(barrier, inc=1, device_id=where, device_id_type=MESH)
 
     loads = [
         pltpu.make_async_copy(src, dst, in_sems.at[n])
@@ -73,13 +88,14 @@
 
     sent = []
 
-    def remote(src, dst, ssem, rsem, where, start=True):
+    def remote(src, dst, ssem, rsem, where, start=True, log=True):
         copy = pltpu.make_async_remote_copy(
             src_ref=src, dst_ref=dst, send_sem=ssem, recv_sem=rsem, device_id=where, device_id_type=MESH
         )
         if start:
             copy.start()
-        sent.append(copy)
+        if log:
+            sent.append(copy)
         return copy
 
     lane = lax.broadcasted_iota(jnp.int32, (1, 128), 1)
@@ -88,7 +104,7 @@
     for o in range(own_filt):
         shard_stage[:, :, o, :] = shard_raw[0, o].astype(F32)
     shard_ref[...] = shard_stage[...].reshape(shard_rows, 128).astype(BF16)
-    grads[0, chan] = shard_ref[...]
+    grads[0, chan, inner_rows] = shard_ref[...]
     loads[1].wait()
     for i in range(32):
         act_stage[:, :, i, :] = act_raw[i].astype(F32)
@@ -107,42 +123,65 @@
             pieces.append(jnp.concatenate(pair, axis=1))
         taps_ref[block] = jnp.concatenate(pieces, axis=0).astype(BF16)
     acc[...] = jnp.zeros(acc.shape, F32)
-    pl.semaphore_wait(barrier, len(partners) + rank)
-
-    over, wover = {}, {}
-    for d in range(1, nf):
-        target, target_rank = filt_at(d)
-        over[d] = remote(
-            shard_ref, grads.at[d, chan], s_filt.at[d - 1], r_filt.at[d - 1], {"filt": target}, start=False
+    pl.semaphore_wait(barrier, len(partners) + filt * jnp.where(at_end, 2, 1))
+
+    over, wover, edge = {}, {}, {}
+    for d in range(nf):
+        target = filt_at(d)
+        edge[d] = remote(
+            shard_ref.at[layers(edge_from)], grads.at[d, chan, layers(edge_to)],
+            s_edge.at[d], r_edge.at[d], {"filt": target, "space": across}, start=False, log=False,
         )
-        wover[d] = remote(
-            taps_ref.at[target, pl.ds(pl.multiple_of(row * w_rows, w_rows), w_rows)],
-            wparts.at[row, d - 1], s_wf.at[d - 1], r_wf.at[d - 1], {"filt": target}, start=False,
-        )
-
-    def send_back(d):
-        target, target_rank = filt_at(d)
-
-        @pl.when(rank > target_rank)
+        if d > 0:
+            over[d] = remote(
+                shard_ref, grads.at[d, chan, inner_rows], s_filt.at[d - 1], r_filt.at[d - 1],
+                {"filt": target}, start=False,
+            )
+            wover[d] = remote(
+                taps_ref.at[target, pl.ds(pl.multiple_of(w_mine * w_rows, w_rows), w_rows)],
+                wparts.at[w_mine, d - 1], s_wf.at[d - 1], r_wf.at[d - 1], {"filt": target}, start=False,
+            )
+
+    def send_over(d):
+        wover[d].start()
+        over[d].start()
+        pl.when(at_end)(edge[d].start)
+
+    def tell(d):
+        target = filt_at(d)
+
+        @pl.when(filt > target)
         def _():
-            pl.semaphore_signal(told.at[d - 1], inc=1, device_id={"filt": target}, device_id_type=MESH)
-            over[d].start()
-            wover[d].start()
+            pl.semaphore_signal(told.at[d - 1, 0], inc=1, device_id={"filt": target}, device_id_type=MESH)
+
+            @pl.when(at_end)
+            def _():
+                where = {"filt": target, "space": across}
+                pl.semaphore_signal(told.at[d - 1, 1], inc=1, device_id=where, device_id_type=MESH)
+
+    def send_back(d, who):
+        pl.when(filt == who)(lambda: send_over(d))
 
     def send_on(d, who):
-        target, target_rank = filt_at(d)
-
         @pl.when(functools.reduce(jnp.logical_or, [filt == w for w in who]))
         def _():
-            pl.semaphore_wait(told.at[nf - d - 1], 1)
-            over[d].start()
-            wover[d].start()
-
-    send_back(2)
-    send_back(1)
-    send_back(3)
+            pl.semaphore_wait(told.at[nf - d - 1, 0], 1)
+
+            @pl.when(at_end)
+            def _():
+                pl.semaphore_wait(told.at[nf - d - 1, 1], 1)
+
+            send_over(d)
+
+    for d in (2, 1, 3):
+        tell(d)
+    for d in range(1, nf):
+        send_back(d, nf - d)
+    pl.when(at_end)(edge[0].start)
     own = [
-        remote(shard_ref, grads.at[0, chan], s_own.at[d - 1], r_own.at[d - 1], {"chan": (chan + d) % nc})
+        remote(
+            shard_ref, grads.at[0, chan, inner_rows], s_own.at[d - 1], r_own.at[d - 1], {"chan": (chan + d) % nc}
+        )
         for d in range(1, nc)
     ]
     up = remote(acts.at[4, pl.ds(1, 4)], acts.at[0, pl.ds(1, 4)], s_act.at[0], r_act.at[0], {"space": after})
@@ -171,7 +210,7 @@
         x, z = h // 2, (h % 2) * 2
         start = pl.multiple_of(h * 2 * own_filt, 2 * own_filt)
         columns = []
-        for g in pair_of(grads[0, :, pl.ds(start, 2 * own_filt), :]):
+        for g in pair_of(grads[0, :, pl.ds(start + layer_rows, 2 * own_filt), :]):
             low = jnp.where(last, 0.0, pltpu.roll(g, 127, 1))
             high = jnp.where(first, 0.0, pltpu.roll(g, 1, 1))
             columns.append(jnp.concatenate([low, g, high], axis=0).astype(BF16))
@@ -198,29 +237,46 @@
             remote(mine.at[pl.ds(theirs, y_rows)], from_y.at[d - 1], s_yr.at[d - 1], r_yr.at[d - 1], at_y(d))
         )
 
-    x_copies, sib_copies = {}, {}
+    passed, passed_edge = {}, {}
+
+    def pass_edge(d):
+        for e in range(1, nc):
+            block = grads.at[d, chan, layers(edge_in)]
+            passed_edge[d, e] = remote(
+                block, block, s_pe.at[d, e - 1], r_pe.at[d, e - 1], {"chan": (chan + e) % nc}, start=False, log=False
+            )
+
+        @pl.when(at_end)
+        def _():
+            edge[d].wait_recv()
+            for e in range(1, nc):
+                passed_edge[d, e].start()
 
     def forward(d):
         over[d].wait_recv()
-        for e in range(1, nx):
-            x_copies[d, e] = remote(
-                grads.at[d, chan], grads.at[d, chan], s_x.at[d - 1, e - 1], r_x.at[d - 1, e - 1], at_x(e)
+        for e in range(1, nc):
+            block = grads.at[d, chan, inner_rows]
+            passed[d, e] = remote(
+                block, block, s_pass.at[d - 1, e - 1], r_pass.at[d - 1, e - 1], {"chan": (chan + e) % nc}
             )
-        sib_copies[d, 0] = remote(
-            grads.at[d, chan], grads.at[d, chan], s_sib.at[d - 1, 0], r_sib.at[d - 1, 0], {"chan": sib}
-        )
-
-    def share(d):
-        for e in range(1, nx):
-            x_copies[d, e].wait_recv()
-            source = ((chip + nx - e) % nx) * 2 + core
-            sib_copies[d, e] = remote(
-                grads.at[d, source], grads.at[d, source], s_sib.at[d - 1, e], r_sib.at[d - 1, e], {"chan": sib}
-            )
-
-    send_on(1, (1,))
-    send_on(3, (3,))
+        pass_edge(d)
+
+    def take(which):
+        for (d, e), copy in passed.items():
+            if d in which:
+                copy.wait_recv()
+
+        @pl.when(at_end)
+        def _():
+            for (d, e), copy in passed_edge.items():
+                if d in which:
+                    copy.wait_recv()
+
+    for d, who in ((3, 2), (2, 3), (3, 3)):
+        send_back(d, who)
+    send_on(1, (1, 2))
     send_on(2, (1,))
+    pass_edge(0)
 
     mine_y = pl.multiple_of(row * y_rows, y_rows)
     for copy in y_red:
@@ -238,6 +294,21 @@
 
     send_on(1, (0,))
     send_on(3, (0,))
+    wshare = {}
+
+    def share_weights(d):
+        wover[d].wait_recv()
+        block = wparts.at[w_mine, d - 1]
+        for e in range(1, 2 * ny):
+            wshare[d, e] = remote(block, block, s_wy.at[d - 1, e - 1], r_wy.at[d - 1, e - 1], at_w(e))
+
+    def widen(out, column, a, b):
+        a = a.astype(F32)
+        b = jnp.zeros_like(a) if b is None else b.astype(F32)
+        columns = slice(column, column + 128)
+        out[0:128, columns] = jnp.where(lane < 64, a, pltpu.roll(b, 64, 1)).astype(BF16)
+        out[128:256, columns] = jnp.where(lane < 64, pltpu.roll(a, 64, 1), b).astype(BF16)
+
     forward(1)
     forward(3)
 
@@ -252,33 +323,19 @@
         remote(total.at[place], total.at[place], s_zg.at[d - 1], r_zg.at[d - 1], at_z(d)) for d in range(1, nz)
     ]
     send_on(2, (0,))
-    share(1)
-    share(3)
-    for d in range(1, nf):
-        wover[d].wait_recv()
-    wshare = [
-        remote(wparts.at[row], wparts.at[row], s_wy.at[d - 1], r_wy.at[d - 1], at_y(d)) for d in range(1, ny)
-    ]
+    share_weights(1)
+    share_weights(3)
     forward(2)
-
-    for copy in wshare:
-        copy.wait_recv()
-    blocks = [taps_ref[filt].astype(F32)]
-    blocks += [wparts[:, d].reshape(TAP_ROWS, 128).astype(F32) for d in (0, 2, 1)]
-    for i in range(0, nf, 2):
-        a, b = blocks[i], blocks[i + 1]
-        lhs[0:128, i * 64 : i * 64 + 128] = jnp.where(lane < 64, a, pltpu.roll(b, 64, 1)).astype(BF16)
-        lhs[128:256, i * 64 : i * 64 + 128] = jnp.where(lane < 64, pltpu.roll(a, 64, 1), b).astype(BF16)
-
-    share(2)
-    for copy in z_gat:
-        copy.wait_recv()
-    place_y = pl.ds(mine_y, y_rows)
-    y_gat = [
-        remote(total.at[place_y], total.at[place_y], s_yg.at[d - 1], r_yg.at[d - 1], at_y(d)) for d in range(1, ny)
-    ]
-
-    def product(which, columns, add):
+    share_weights(2)
+    for (d, e), copy in wshare.items():
+        if d != 2:
+            copy.wait_recv()
+    widen(lhs, 0, taps_ref[filt], wparts[:, 0].reshape(TAP_ROWS, 128))
+    widen(lhs, 128, wparts[:, 2].reshape(TAP_ROWS, 128), None)
+    lowest = jnp.where(jnp.logical_and(at_low, space > 0), 0, 2)
+    highest = jnp.where(jnp.logical_and(at_high, space < ns - 1), 12, 10)
+
+    def product(which, left, add):
         def step(h, carry):
             x, z = h // 2, (h % 2) * 2
             start = pl.multiple_of(h * 2 * own_filt, 2 * own_filt)
@@ -286,22 +343,29 @@
             rhs = jnp.concatenate(
                 [jnp.concatenate([p[i] for p in parts], axis=0) for i in range(2)], axis=1
             ).astype(BF16)
-            result = jnp.dot(lhs[:, columns], rhs, preferred_element_type=F32)
+            result = jnp.dot(left[:, 0 : 64 * len(which)], rhs, preferred_element_type=F32)
             for i in range(2):
                 half = result[:, i * 128 : i * 128 + 128]
-                prod[x + 2, z + 1 + i] = prod[x + 2, z + 1 + i] + half if add else half
+                prod[x + 1, z + 1 + i] = prod[x + 1, z + 1 + i] + half if add else half
             return carry
 
-        lax.fori_loop(0, 8, step, 0)
-
-    for (d, e), copy in sib_copies.items():
-        if d != 2:
-            copy.wait_recv()
-    product((0, 1, 3), slice(0, 192), False)
-    for (d, e), copy in sib_copies.items():
+        lax.fori_loop(lowest, highest, step, 0)
+
+    take((0, 1, 3))
+    product((0, 1, 3), lhs, False)
+    for copy in z_gat:
+        copy.wait_recv()
+    place_y = pl.ds(mine_y, y_rows)
+    y_gat = [
+        remote(total.at[place_y], total.at[place_y], s_yg.at[d - 1], r_yg.at[d - 1], at_y(d)) for d in range(1, ny)
+    ]
+
+    for (d, e), copy in wshare.items():
         if d == 2:
             copy.wait_recv()
-    product((2,), slice(192, 256), True)
+    widen(late, 0, wparts[:, 1].reshape(TAP_ROWS, 128), None)
+    take((2,))
+    product((2,), late, True)
 
     def sum_step(n, x):
         z = n
@@ -323,10 +387,22 @@
         for n in range(4):
             sum_step(n, x)
 
-    layer(0)
-    low_out = remote(outs.at[0], halo.at[1], s_halo.at[0], r_halo.at[0], {"space": before})
-    layer(5)
-    high_out = remote(outs.at[5], halo.at[0], s_halo.at[1], r_halo.at[1], {"space": after})
+    low_out = remote(
+        outs.at[0], halo.at[1], s_halo.at[0], r_halo.at[0], {"space": before}, start=False, log=False
+    )
+    high_out = remote(
+        outs.at[5], halo.at[0], s_halo.at[1], r_halo.at[1], {"space": after}, start=False, log=False
+    )
+
+    @pl.when(jnp.logical_not(at_low))
+    def _():
+        layer(0)
+        low_out.start()
+
+    @pl.when(jnp.logical_not(at_high))
+    def _():
+        layer(5)
+        high_out.start()
 
     def inner(x, carry):
         layer(x)
@@ -347,13 +423,26 @@
                 src = 288 + (at if at < 144 else at - 144)
                 gw_ref[(a * 3 + 2) * 3 + c, half * 16 : half * 16 + 16] = total[src : src + 16, left : left + 64]
 
-    low_out.wait_recv()
-    high_out.wait_recv()
-    outs[1] = outs[1] + jnp.where(space > 0, halo[0], 0.0)
-    outs[4] = outs[4] + jnp.where(space < ns - 1, halo[1], 0.0)
+    @pl.when(jnp.logical_not(at_low))
+    def _():
+        high_out.wait_recv()
+        outs[1] = outs[1] + halo[0]
+        low_out.wait_send()
+
+    @pl.when(jnp.logical_not(at_high))
+    def _():
+        low_out.wait_recv()
+        outs[4] = outs[4] + halo[1]
+        high_out.wait_send()
+
     gi_ref[...] = outs[1:5].reshape(128, 128).astype(BF16)
     for copy in sent:
         copy.wait_send()
+
+    @pl.when(at_end)
+    def _():
+        for copy in list(edge.values()) + list(passed_edge.values()):
+            copy.wait_send()
 
 
 def body(sizes, activations, out_grad, weight):
@@ -368,7 +457,7 @@
     z_rows = y_rows // nz
     pairs = []
     for shape in (
-        (nc - 1,), (2,), (nf - 1,), (nf - 1,), (ny - 1,), (nf - 1, max(nx - 1, 1)), (nf - 1, nx),
+        (nc - 1,), (2,), (nf - 1,), (nf - 1,), (nf - 1, 2 * ny - 1), (nf - 1, nc - 1), (nf,), (nf, nc - 1),
         (ny - 1,), (nz - 1,), (nz - 1,), (ny - 1,), (2,),
     ):
         pairs += [dma(shape), dma(shape)]
@@ -389,11 +478,12 @@
             pltpu.VMEM((16 * own_filt, 128), BF16),
             pltpu.VMEM((nf, TAP_ROWS, 128), BF16),
             dma((3,)),
-            pltpu.SemaphoreType.REGULAR((nf - 1,)),
-            pltpu.VMEM((nf, nc, 16 * own_filt, 128), BF16),
+            pltpu.SemaphoreType.REGULAR((nf - 1, 2)),
+            pltpu.VMEM((nf, nc, 24 * own_filt, 128), BF16),
             pltpu.VMEM((6, 6, 32, 128), BF16),
-            pltpu.VMEM((ny, nf - 1, TAP_ROWS // ny, 128), BF16),
+            pltpu.VMEM((2 * ny, nf - 1, TAP_ROWS // (2 * ny), 128), BF16),
             pltpu.VMEM((256, 256), BF16),
+            pltpu.VMEM((256, 128), BF16),
             pltpu.VMEM((288, 256), F32),
             pltpu.VMEM((ROWS, 128), F32),
             pltpu.VMEM((ny - 1, y_rows, 128), F32),
@@ -405,7 +495,7 @@
             pltpu.VMEM((2, 4, 8, 128), F32),
         ] + pairs,
         compiler_params=pltpu.CompilerParams(
-            collective_id=0, has_side_effects=True, vmem_limit_bytes=32 * 1024 * 1024
+            collective_id=0, has_side_effects=True, vmem_limit_bytes=63 * 1024 * 1024
         ),
     )(activations, out_grad, weight)
     return jnp.transpose(gi.reshape(4, 4, 8, 128), (2, 0, 1, 3)), gw

time: 69.4 us -> 62.7 us (0.903)
  the two profiles are of different devices: /device:TPU:1 before, /device:TPU:4 now
where the time goes in v3:
time: 62.7 us; the launch traced here: 62.5 us
  Pallas kernels  58.6 us (93%)
  local copies, waits for them, and re-layouts  3.19 us (5%)
  between operations  0.64 us (1%)
    pallas_call x1, Pallas kernels, body(): pl.pallas_call(functools.partial(kernel, sizes, 1.0 / math.sqrt(cells)),...  58.6 us
    unnamed x1, local copies, waits for them, and re-layouts  1.8 us
    reshape x1, local copies, waits for them, and re-layouts, body(): return (jnp.transpose(gi.reshape(4, 4, 8, 128), (2, 0, 1, 3)), gw)  1.39 us

profile of v3, /device:TPU:4, one launch (start us, length us, event | category | flops | bytes accessed | tf_op | source)
XLA Modules:
  0.0 62.5 jit_solution(14169258846712652851)
XLA Ops:
  0.6 58.6 %shard_map.50 = (bf16[128,128]{1,0:T(8,128)(2,1)}, f32[27,32,64]{2,1,0:T(8,128)}) custom-call(bf16[32,4,4,128]{3,2,1,0:T(4,128)(2,1)} %act_hbm.1, bf16[1,8,4,4,128]{4,3,2,1,0:T(4,128)(2,1)} %shard_hbm.1, bf16[27,32,64]{2,1,0:T(8,128)(2,1)} %weight_hbm.1), custom_call_target="tpu_custom_call" | custom-call | tf_op jit(solution)/shard_map/pallas_call | solution.py:464
  59.3 1.4 %copy.7 = bf16[4,4,8,128]{3,1,0,2:T(4,128)(2,1)} copy(bf16[4,4,8,128]{3,2,1,0:T(8,128)(2,1)} %bitcast.5) | data formatting | bytes 65536 | tf_op jit(solution)/shard_map/reshape | solution.py:501
  60.7 1.8 %copy.9 = f32[27,32,64]{2,1,0:T(8,128)} copy(f32[27,32,64]{2,1,0:T(8,128)} %get-tuple-element.9) | data formatting | bytes 442368

commit v4 on v3

--- a/solution.py
+++ b/solution.py
@@ -145,7 +145,7 @@
     def send_over(d):
         wover[d].start()
         over[d].start()
-        pl.when(at_end)(edge[d].start)
+        pl.when(at_end)(lambda: edge[d].start())
 
     def tell(d):
         target = filt_at(d)
@@ -325,8 +325,15 @@
     send_on(2, (0,))
     share_weights(1)
     share_weights(3)
+    share_weights(2)
     forward(2)
-    share_weights(2)
+    for copy in z_gat:
+        copy.wait_recv()
+    place_y = pl.ds(mine_y, y_rows)
+    y_gat = [
+        remote(total.at[place_y], total.at[place_y], s_yg.at[d - 1], r_yg.at[d - 1], at_y(d)) for d in range(1, ny)
+    ]
+
     for (d, e), copy in wshare.items():
         if d != 2:
             copy.wait_recv()
@@ -335,7 +342,7 @@
     lowest = jnp.where(jnp.logical_and(at_low, space > 0), 0, 2)
     highest = jnp.where(jnp.logical_and(at_high, space < ns - 1), 12, 10)
 
-    def product(which, left, add):
+    def product(which, left, add, steps):
         def step(h, carry):
             x, z = h // 2, (h % 2) * 2
             start = pl.multiple_of(h * 2 * own_filt, 2 * own_filt)
@@ -349,23 +356,17 @@
                 prod[x + 1, z + 1 + i] = prod[x + 1, z + 1 + i] + half if add else half
             return carry
 
-        lax.fori_loop(lowest, highest, step, 0)
+        lax.fori_loop(*steps, step, 0)
 
     take((0, 1, 3))
-    product((0, 1, 3), lhs, False)
-    for copy in z_gat:
-        copy.wait_recv()
-    place_y = pl.ds(mine_y, y_rows)
-    y_gat = [
-        remote(total.at[place_y], total.at[place_y], s_yg.at[d - 1], r_yg.at[d - 1], at_y(d)) for d in range(1, ny)
-    ]
-
+    product((0, 1, 3), lhs, False, (lowest, highest))
     for (d, e), copy in wshare.items():
         if d == 2:
             copy.wait_recv()
     widen(late, 0, wparts[:, 1].reshape(TAP_ROWS, 128), None)
     take((2,))
-    product((2,), late, True)
+    product((2,), late, True, (2, 4))
+    product((2,), late, True, (8, 10))
 
     def sum_step(n, x):
         z = n
@@ -404,6 +405,9 @@
         layer(5)
         high_out.start()
 
+    for steps in ((lowest, 2), (4, 8), (10, highest)):
+        product((2,), late, True, steps)
+
     def inner(x, carry):
         layer(x)
         return carry
@@ -435,7 +439,8 @@
         outs[4] = outs[4] + halo[1]
         high_out.wait_send()
 
-    gi_ref[...] = outs[1:5].reshape(128, 128).astype(BF16)
+    for i in range(8):
+        gi_ref[i] = outs[1:5, :, i, :].astype(BF16)
     for copy in sent:
         copy.wait_send()
 
@@ -443,6 +448,24 @@
     def _():
         for copy in list(edge.values()) + list(passed_edge.values()):
             copy.wait_send()
+
+
+def hand_over(gi_in, gw_in, gi_out, gw_out, gi_mid, gw_mid, sems):
+    loads = [
+        pltpu.make_async_copy(gw_in, gw_mid, sems.at[0]),
+        pltpu.make_async_copy(gi_in, gi_mid, sems.at[1]),
+    ]
+    stores = [
+        pltpu.make_async_copy(gw_mid, gw_out, sems.at[2]),
+        pltpu.make_async_copy(gi_mid, gi_out, sems.at[3]),
+    ]
+    for load in loads:
+        load.start()
+    for load, store in zip(loads, stores):
+        load.wait()
+        store.start()
+    for store in stores:
+        store.wait()
 
 
 def body(sizes, activations, out_grad, weight):
@@ -464,7 +487,7 @@
     gi, gw = pl.pallas_call(
         functools.partial(kernel, sizes, 1.0 / math.sqrt(cells)),
         out_shape=(
-            jax.ShapeDtypeStruct((128, 128), BF16),
+            jax.ShapeDtypeStruct((8, 4, 4, 128), BF16),
             jax.ShapeDtypeStruct((27, 32, 64), F32),
         ),
         in_specs=[hbm] * 3,
@@ -498,7 +521,18 @@
             collective_id=0, has_side_effects=True, vmem_limit_bytes=63 * 1024 * 1024
         ),
     )(activations, out_grad, weight)
-    return jnp.transpose(gi.reshape(4, 4, 8, 128), (2, 0, 1, 3)), gw
+    return tuple(
+        pl.pallas_call(
+            hand_over,
+            out_shape=(
+                jax.ShapeDtypeStruct((8, 4, 4, 128), BF16),
+                jax.ShapeDtypeStruct((27, 32, 64), F32),
+            ),
+            in_specs=[hbm, hbm],
+            out_specs=(hbm, hbm),
+            scratch_shapes=[pltpu.VMEM((8, 4, 4, 128), BF16), pltpu.VMEM((27, 32, 64), F32), dma((4,))],
+        )(gi, gw)
+    )
 
 
 def solution(mesh):

time: 62.7 us -> 59.8 us (0.954)
  the two profiles are of different devices: /device:TPU:4 before, /device:TPU:6 now
where the time goes in v4:
time: 59.8 us; the launch traced here: 59.6 us
  Pallas kernels  59 us (99%)
  between operations  0.64 us (1%)
    pallas_call x1, Pallas kernels, body(): pl.pallas_call(functools.partial(kernel, sizes, 1.0 / math.sqrt(cells)),...  57.2 us
    pallas_call x1, Pallas kernels, body(): pl.pallas_call(hand_over, out_shape=(jax.ShapeDtypeStruct((8, 4, 4, 128),...  1.81 us

profile of v4, /device:TPU:6, one launch (start us, length us, event | category | flops | bytes accessed | tf_op | source)
XLA Modules:
  0.0 59.6 jit_solution(17237072645977583179)
XLA Ops:
  0.6 57.2 %shard_map.50 = (bf16[8,4,4,128]{3,2,1,0:T(4,128)(2,1)}, f32[27,32,64]{2,1,0:T(8,128)}) custom-call(bf16[32,4,4,128]{3,2,1,0:T(4,128)(2,1)} %act_hbm.1, bf16[1,8,4,4,128]{4,3,2,1,0:T(4,128)(2,1)} %shard_hbm.1, bf16[27,32,64]{2,1,0:T(8,128)(2,1)} %weight_hbm.1), custom_call_target="tpu_custom_call" | custom-call | tf_op jit(solution)/shard_map/pallas_call | solution.py:487
  57.8 1.8 %shard_map.51 = (bf16[8,4,4,128]{3,2,1,0:T(4,128)(2,1)}, f32[27,32,64]{2,1,0:T(8,128)}) custom-call(bf16[8,4,4,128]{3,2,1,0:T(4,128)(2,1)} %get-tuple-element.4.gi_in, f32[27,32,64]{2,1,0:T(8,128)} %get-tuple-element.5.gw_in), custom_call_target="tpu_custom_call" | custom-call | tf_op jit(solution)/shard_map/pallas_call | solution.py:525

commit v5 on v4

--- a/solution.py
+++ b/solution.py
@@ -17,8 +17,8 @@
 def kernel(
     sizes, scale,
     act_hbm, shard_hbm, weight_hbm,
-    gi_ref, gw_ref,
-    act_raw, shard_raw, weight_raw, act_stage, shard_stage, shard_ref, taps_ref, in_sems, told,
+    gi_ref, gw_hbm,
+    gw_ref,    act_raw, shard_raw, weight_raw, act_stage, shard_stage, shard_ref, taps_ref, in_sems, told,
     grads, acts, wparts, lhs, late, acc, mine, from_y, for_z, from_z, total, prod, outs, halo,
     s_own, r_own, s_act, r_act, s_filt, r_filt, s_wf, r_wf, s_wy, r_wy, s_pass, r_pass, s_edge, r_edge, s_pe, r_pe,
     s_yr, r_yr, s_zr, r_zr, s_zg, r_zg, s_yg, r_yg, s_halo, r_halo,
@@ -61,10 +61,10 @@
         return (filt + d) % nf
 
     barrier = pltpu.get_barrier_semaphore()
-    partners = [{"chan": (chan + d) % nc} for d in range(1, nc)]
-    partners += [at_y(d) for d in range(1, ny)] + [at_z(d) for d in range(1, nz)]
-    partners += [{"space": before}, {"space": after}]
-    partners += [at_w(2 * e + 1) for e in range(1, ny)]
+    partners = [{"space": before}, {"space": after}]
+    partners += [at_z(d) for d in (4, 3, 5, 2, 6, 1, 7) if d < nz]
+    partners += [at_w(2 * e + 1) for e in range(1, ny)] + [at_y(d) for d in range(1, ny)]
+    partners += [{"chan": (chan + d) % nc} for d in range(1, nc)]
     for partner in partners:
         pl.semaphore_signal(barrier, inc=1, device_id=partner, device_id_type=MESH)
     for d in range(1, nf):
@@ -427,6 +427,8 @@
                 src = 288 + (at if at < 144 else at - 144)
                 gw_ref[(a * 3 + 2) * 3 + c, half * 16 : half * 16 + 16] = total[src : src + 16, left : left + 64]
 
+    gw_store = pltpu.make_async_copy(gw_ref, gw_hbm, in_sems.at[3])
+    gw_store.start()
     @pl.when(jnp.logical_not(at_low))
     def _():
         high_out.wait_recv()
@@ -443,6 +445,7 @@
         gi_ref[i] = outs[1:5, :, i, :].astype(BF16)
     for copy in sent:
         copy.wait_send()
+    gw_store.wait()
 
     @pl.when(at_end)
     def _():
@@ -491,8 +494,9 @@
             jax.ShapeDtypeStruct((27, 32, 64), F32),
         ),
         in_specs=[hbm] * 3,
-        out_specs=(vmem, vmem),
+        out_specs=(vmem, hbm),
         scratch_shapes=[
+            pltpu.VMEM((27, 32, 64), F32),
             pltpu.VMEM(activations.shape, BF16),
             pltpu.VMEM(out_grad.shape, BF16),
             pltpu.VMEM(weight.shape, BF16),
@@ -500,7 +504,7 @@
             pltpu.VMEM((4, 4, own_filt, 128), F32),
             pltpu.VMEM((16 * own_filt, 128), BF16),
             pltpu.VMEM((nf, TAP_ROWS, 128), BF16),
-            dma((3,)),
+            dma((4,)),
             pltpu.SemaphoreType.REGULAR((nf - 1, 2)),
             pltpu.VMEM((nf, nc, 24 * own_filt, 128), BF16),
             pltpu.VMEM((6, 6, 32, 128), BF16),

time: 59.8 us -> 60.1 us (level)
  no operation moved by 1% of the time
where the time goes in v5:
time: 60.1 us; the launch traced here: 59.9 us
  Pallas kernels  59.3 us (99%)
  between operations  0.64 us (1%)
    pallas_call x1, Pallas kernels, body(): pl.pallas_call(functools.partial(kernel, sizes, 1.0 / math.sqrt(cells)),...  57.5 us
    pallas_call x1, Pallas kernels, body(): pl.pallas_call(hand_over, out_shape=(jax.ShapeDtypeStruct((8, 4, 4, 128),...  1.81 us

profile of v5, /device:TPU:6, one launch (start us, length us, event | category | flops | bytes accessed | tf_op | source)
XLA Modules:
  0.0 59.9 jit_solution(8718765667165713562)
XLA Ops:
  0.6 57.5 %shard_map.50 = (bf16[8,4,4,128]{3,2,1,0:T(4,128)(2,1)}, f32[27,32,64]{2,1,0:T(8,128)}) custom-call(bf16[32,4,4,128]{3,2,1,0:T(4,128)(2,1)} %act_hbm.1, bf16[1,8,4,4,128]{4,3,2,1,0:T(4,128)(2,1)} %shard_hbm.1, bf16[27,32,64]{2,1,0:T(8,128)(2,1)} %weight_hbm.1), custom_call_target="tpu_custom_call" | custom-call | tf_op jit(solution)/shard_map/pallas_call | solution.py:490
  58.1 1.8 %shard_map.51 = (bf16[8,4,4,128]{3,2,1,0:T(4,128)(2,1)}, f32[27,32,64]{2,1,0:T(8,128)}) custom-call(bf16[8,4,4,128]{3,2,1,0:T(4,128)(2,1)} %get-tuple-element.4.gi_in, f32[27,32,64]{2,1,0:T(8,128)} %get-tuple-element.5.gw_in), custom_call_target="tpu_custom_call" | custom-call | tf_op jit(solution)/shard_map/pallas_call | solution.py:529
